TPU v7x, 128 devices: a whole 4x4x4 slice. The times are simulated.
128 devices in a mesh: kpt: 16 (over z, y_hi, core), row: 8 (over x, y_lo).
Axes of the slice: x: 4, y: 4 (y_hi: 2, y_lo: 2; y = y_hi * 2 + y_lo), z: 4, core: 2. Of those that a mesh axis runs over, the one named last changes fastest.
Arguments:
- occ_orbitals: bfloat16 [64, 2048, 128], P('kpt', 'row'), may hold values from -0.5 to 0.5
- virt_orbitals: bfloat16 [64, 2048, 256], P('kpt', 'row'), may hold values from -0.375 to 0.375
- occ_gap: bfloat16 [64, 128], P('kpt'), may hold values from 0.049804688 to 3
- virt_gap: bfloat16 [64, 256], P('kpt'), may hold values from 0.049804688 to 3
- partner: int32 [3, 64], replicated, may hold values from 0 to 63, as said below
Outputs:
- chi: float32 [3, 4, 2048, 2048], P(None, None, 'row', 'kpt')
Inputs may be any that keep to these rules, and one draw needn't show every extreme that they name: For each transfer q there is a shift s_q of 0 to 4 with partner[q, k] = (k - s_q) mod 64 for every k; the shifts of different transfers differ, and some transfer has s_q = 4.
All inputs are finite; a program needn't handle non-finite values.
Results may differ from a plain program's by a relative error of at most 0.0003.
Values may be sent and summed in bfloat16 or wider, within the bound.
No kernel may reach another device: no remote copies, remote signals or barrier semaphores. Data moves between devices by JAX's collectives and lax.ppermute only.
A program may use at most 320 MiB of HBM per device.

v0:
```python
import jax
import jax.numpy as jnp
from jax import lax
from jax.sharding import PartitionSpec as P

NTAU = 4


def shifted(block, axis, distance):
    devices = range(lax.axis_size(axis))
    route = [((i - distance) % len(devices), i) for i in devices]
    return lax.ppermute(block, axis, route)


def weighted(orbitals, energy_gap, moment):
    factor = jnp.exp(-energy_gap.astype(jnp.float32) * moment)
    return (orbitals.astype(jnp.float32) * factor[:, None, :]).astype(jnp.bfloat16)


def greens(row_panel, column_panel):
    return jnp.einsum("kri,kci->krc", row_panel, column_panel, preferred_element_type=jnp.float32)


def on_device(occ_orbitals, virt_orbitals, occ_gap, virt_gap, partner):
    local_count = occ_orbitals.shape[0]
    transfers = partner.shape[0]
    device_k = lax.axis_index("kpt")
    kpt_count = lax.axis_size("kpt")
    total_count = local_count * kpt_count
    tau_values = 0.25 * 2.0 ** jnp.arange(NTAU, dtype=jnp.float32)
    earlier, earlier_gap = shifted((virt_orbitals, virt_gap), "kpt", 1)
    window = jnp.concatenate([earlier, virt_orbitals], axis=0)
    window_gap = jnp.concatenate([earlier_gap, virt_gap], axis=0)
    occ_points, window_points = (
        lax.all_gather(occ_orbitals, "row", axis=1, tiled=True),
        lax.all_gather(window, "row", axis=1, tiled=True),
    )
    window_start = (device_k - 1) % kpt_count * local_count
    own_partners = lax.dynamic_slice_in_dim(partner, device_k * local_count, local_count, 1)
    window_slots = (own_partners - window_start) % total_count
    blocks = []
    for step_index in range(NTAU):
        moment = tau_values[step_index]
        occ_green = greens(weighted(occ_orbitals, occ_gap, moment), occ_points)
        window_green = greens(weighted(window, window_gap, moment), window_points)
        sums_here = []
        for transfer in range(transfers):
            virt_green = jnp.take(window_green, window_slots[transfer], axis=0)
            sums_here.append(jnp.sum(occ_green * virt_green, axis=0))
        blocks.append(jnp.stack(sums_here))
    partial_chi = jnp.stack(blocks, axis=1)
    return lax.psum_scatter(partial_chi, "kpt", scatter_dimension=3, tiled=True)


def solution(mesh):
    in_specs = (P("kpt", "row", None), P("kpt", "row", None), P("kpt", None), P("kpt", None), P())
    out_specs = P(None, None, "row", "kpt")
    return jax.shard_map(
        on_device, mesh=mesh, in_specs=in_specs, out_specs=out_specs, check_vma=False
    )
```

profile of v0, /device:TPU:0, one launch (start us, length us, event | category | flops | bytes accessed | tf_op | source)
XLA Modules:
  0.0 672.6 jit_solution(10902497259233163905)
XLA Ops:
  7.4 13.3 %collective-permute-done = bf16[4,256,256]{2,1,0:T(8,128)(2,1)S(1)} collective-permute-done((bf16[4,256,256]{2,1,0:T(8,128)(2,1)}, bf16[4,256,256]{2,1,0:T(8,128)(2,1)S(1)}, u32[]{:S(2)}, u32[]{:S(2)}) %collective-permute-start) | collective-permute-done | bytes 524320 | tf_op jit(solution)/shard_map/ppermute | solution.py:12
  20.7 1.1 constant_dynamic-update-slice_fusion
  24.3 3.1 multiply_exponential_fusion.5
  27.4 2.3 collective-permute-done.1
  29.7 3.1 multiply_exponential_fusion.1
  32.8 29.8 %all-gather.3.cloned.1.call-done = bf16[4,2048,128]{2,1,0:T(8,128)(2,1)} async-done(((bf16[4,256,128]{2,1,0:T(8,128)(2,1)}), bf16[4,2048,128]{2,1,0:T(8,128)(2,1)}) %all-gather.3.cloned.1.call-update) | async-done | bytes 2097168 | tf_op jit(solution)/shard_map/all_gather | solution.py:35
  62.6 6.3 fusion.34
  68.9 4.5 fusion.36
  73.4 4.5 fusion.32
  77.8 4.5 fusion.38
  82.3 151.1 %all-gather.5.cloned.1.call-done = bf16[8,2048,256]{2,1,0:T(8,128)(2,1)} async-done(((bf16[8,256,256]{2,1,0:T(8,128)(2,1)}), bf16[8,2048,256]{2,1,0:T(8,128)(2,1)}) %all-gather.5.cloned.1.call-update) | async-done | bytes 8388624 | tf_op jit(solution)/shard_map/all_gather | solution.py:36
  233.3 11.5 %fusion.16 = f32[8,256,2048]{2,1,0:T(8,128)} fusion(bf16[8,2048,256]{2,1,0:T(8,128)(2,1)} %all-gather.5.cloned.1.call-done, bf16[8,256,256]{2,1,0:T(8,128)(2,1)S(1)} %copy-done.1, f32[8,256]{1,0:T(8,128)S(1)} %get-tuple-element.34), kind=kOutput, calls=%fused_computation.49 | convolution fusion | flops 2149056512 | bytes 26222592 | tf_op jit(solution)/shard_map/kri,kci->krc/dot_general | solution.py:21
  244.8 10.0 %gather_fusion.11 = f32[4,256,2048]{2,1,0:T(8,128)} fusion(f32[8,256,2048]{2,1,0:T(8,128)} %fusion.16, s32[1024]{0:T(1024)S(1)} %get-tuple-element.49), kind=kCustom, calls=%fused_computation.11.clone | custom fusion | bytes 16777232 | tf_op jit(solution)/shard_map/jit(_take)/gather | solution.py:48
  254.9 10.1 %gather_fusion.10 = f32[4,256,2048]{2,1,0:T(8,128)} fusion(f32[8,256,2048]{2,1,0:T(8,128)} %fusion.16, s32[1024]{0:T(1024)S(1)} %get-tuple-element.50), kind=kCustom, calls=%fused_computation.10.clone | custom fusion | bytes 16777232 | tf_op jit(solution)/shard_map/jit(_take)/gather | solution.py:48
  265.0 11.5 %fusion.18 = f32[8,256,2048]{2,1,0:T(8,128)} fusion(bf16[8,2048,256]{2,1,0:T(8,128)(2,1)} %all-gather.5.cloned.1.call-done, bf16[8,256,256]{2,1,0:T(8,128)(2,1)S(1)} %copy-done.1, f32[8,256]{1,0:T(8,128)S(1)} %get-tuple-element.33), kind=kOutput, calls=%fused_computation.50 | convolution fusion | flops 2149056512 | bytes 26222592 | tf_op jit(solution)/shard_map/kri,kci->krc/dot_general | solution.py:21
  276.5 10.1 %gather_fusion.8 = f32[4,256,2048]{2,1,0:T(8,128)} fusion(f32[8,256,2048]{2,1,0:T(8,128)} %fusion.18, s32[1024]{0:T(1024)S(1)} %get-tuple-element.49), kind=kCustom, calls=%fused_computation.8.clone | custom fusion | bytes 16777232 | tf_op jit(solution)/shard_map/jit(_take)/gather | solution.py:48
  286.6 10.3 %gather_fusion.7 = f32[4,256,2048]{2,1,0:T(8,128)} fusion(f32[8,256,2048]{2,1,0:T(8,128)} %fusion.18, s32[1024]{0:T(1024)S(1)} %get-tuple-element.50), kind=kCustom, calls=%fused_computation.7.clone | custom fusion | bytes 16777232 | tf_op jit(solution)/shard_map/jit(_take)/gather | solution.py:48
  296.9 10.0 %gather_fusion.9 = f32[4,256,2048]{2,1,0:T(8,128)} fusion(f32[8,256,2048]{2,1,0:T(8,128)} %fusion.16, s32[1024]{0:T(1024)S(1)} %pad_clamp_fusion.2), kind=kCustom, calls=%fused_computation.9.clone | custom fusion | bytes 16777232 | tf_op jit(solution)/shard_map/jit(_take)/gather | solution.py:48
  307.0 10.0 %gather_fusion.6 = f32[4,256,2048]{2,1,0:T(8,128)} fusion(f32[8,256,2048]{2,1,0:T(8,128)} %fusion.18, s32[1024]{0:T(1024)S(1)} %pad_clamp_fusion.2), kind=kCustom, calls=%fused_computation.6.clone | custom fusion | bytes 16777232 | tf_op jit(solution)/shard_map/jit(_take)/gather | solution.py:48
  317.0 11.5 %fusion.22 = f32[8,256,2048]{2,1,0:T(8,128)} fusion(bf16[8,2048,256]{2,1,0:T(8,128)(2,1)} %all-gather.5.cloned.1.call-done, bf16[8,256,256]{2,1,0:T(8,128)(2,1)S(1)} %copy-done.1, f32[8,256]{1,0:T(8,128)S(1)} %get-tuple-element.36), kind=kOutput, calls=%fused_computation.52 | convolution fusion | flops 2149056512 | bytes 26222592 | tf_op jit(solution)/shard_map/kri,kci->krc/dot_general | solution.py:21
  328.5 10.1 %gather_fusion.2 = f32[4,256,2048]{2,1,0:T(8,128)} fusion(f32[8,256,2048]{2,1,0:T(8,128)} %fusion.22, s32[1024]{0:T(1024)S(1)} %get-tuple-element.49), kind=kCustom, calls=%fused_computation.2.clone | custom fusion | bytes 16777232 | tf_op jit(solution)/shard_map/jit(_take)/gather | solution.py:48
  338.6 10.1 %gather_fusion.1 = f32[4,256,2048]{2,1,0:T(8,128)} fusion(f32[8,256,2048]{2,1,0:T(8,128)} %fusion.22, s32[1024]{0:T(1024)S(1)} %get-tuple-element.50), kind=kCustom, calls=%fused_computation.1.clone | custom fusion | bytes 16777232 | tf_op jit(solution)/shard_map/jit(_take)/gather | solution.py:48
  348.6 10.1 %gather_fusion = f32[4,256,2048]{2,1,0:T(8,128)} fusion(f32[8,256,2048]{2,1,0:T(8,128)} %fusion.22, s32[1024]{0:T(1024)S(1)} %pad_clamp_fusion.2), kind=kCustom, calls=%fused_computation.clone | custom fusion | bytes 16777232 | tf_op jit(solution)/shard_map/jit(_take)/gather | solution.py:48
  358.8 11.5 %fusion.20 = f32[8,256,2048]{2,1,0:T(8,128)} fusion(bf16[8,2048,256]{2,1,0:T(8,128)(2,1)} %all-gather.5.cloned.1.call-done, bf16[8,256,256]{2,1,0:T(8,128)(2,1)S(1)} %copy-done.1, f32[8,256]{1,0:T(8,128)S(1)} %get-tuple-element.35), kind=kOutput, calls=%fused_computation.51 | convolution fusion | flops 2149056512 | bytes 26222592 | tf_op jit(solution)/shard_map/kri,kci->krc/dot_general | solution.py:21
  370.3 10.1 %gather_fusion.5 = f32[4,256,2048]{2,1,0:T(8,128)} fusion(f32[8,256,2048]{2,1,0:T(8,128)} %fusion.20, s32[1024]{0:T(1024)S(1)} %get-tuple-element.49), kind=kCustom, calls=%fused_computation.5.clone | custom fusion | bytes 16777232 | tf_op jit(solution)/shard_map/jit(_take)/gather | solution.py:48
  380.3 10.1 %gather_fusion.3 = f32[4,256,2048]{2,1,0:T(8,128)} fusion(f32[8,256,2048]{2,1,0:T(8,128)} %fusion.20, s32[1024]{0:T(1024)S(1)} %pad_clamp_fusion.2), kind=kCustom, calls=%fused_computation.3.clone | custom fusion | bytes 16777232 | tf_op jit(solution)/shard_map/jit(_take)/gather | solution.py:48
  390.4 10.0 %gather_fusion.4 = f32[4,256,2048]{2,1,0:T(8,128)} fusion(f32[8,256,2048]{2,1,0:T(8,128)} %fusion.20, s32[1024]{0:T(1024)S(1)} %get-tuple-element.50), kind=kCustom, calls=%fused_computation.4.clone | custom fusion | bytes 16777232 | tf_op jit(solution)/shard_map/jit(_take)/gather | solution.py:48
  400.5 51.4 %fusion.2 = (f32[256,2048]{1,0:T(8,128)}, f32[256,2048]{1,0:T(8,128)}, f32[256,2048]{1,0:T(8,128)}, f32[256,2048]{1,0:T(8,128)}, f32[256,2048]{1,0:T(8,128)}, /*...) fusion(f32[4,256,2048]{2,1,0:T(8,128)} %fusion.32, ...), kind=kLoop, calls=%fused_computation.18 | loop fusion | flops 69206016 | bytes 159383568 | tf_op jit(solution)/shard_map/reduce_sum | solution.py:49
  451.8 3.4 maximum_bitcast_fusion.3
  459.4 2.1 maximum_bitcast_fusion.2
  461.5 8.5 %pad_maximum_fusion = f32[3,4,256,2048]{3,2,1,0:T(8,128)} fusion(f32[3,1,256,2048]{3,2,1,0:T(8,128)S(1)} %maximum_bitcast_fusion.3, f32[3,1,256,2048]{3,2,1,0:T(8,128)S(1)} %maximum_bitcast_fusion.2, f32[3,1,256,2048]{3,2,1,0:T(8,128)S(1)} %maximum_bitcast_fusion.1, f32[3,1,256,2048]{3,2,1,0:T(8,128)S(1)} %maximum_bitcast_fusion), kind=kLoop, calls=%fused_computation.12 | loop fusion | flops 18874368 | bytes 50331648 | tf_op jit(solution)/shard_map/stack | solution.py:51
  470.1 196.0 %reduce-scatter.2.cloned.1.call-done = f32[3,4,256,128]{3,2,1,0:T(8,128)} async-done(((f32[3,4,256,2048]{3,2,1,0:T(8,128)}), f32[3,4,256,128]{3,2,1,0:T(8,128)}) %reduce-scatter.2.cloned.1.call-update) | async-done | bytes 1572880 | tf_op jit(solution)/shard_map/reduce_scatter | solution.py:52
  (39 shorter events, 7.5 us)
Async XLA Ops:
  6.5 62.4 %copy-start.10 = (bf16[4,256,128]{2,1,0:T(8,128)(2,1)S(1)}, bf16[4,256,128]{2,1,0:T(8,128)(2,1)}, u32[]{:S(2)}) copy-start(bf16[4,256,128]{2,1,0:T(8,128)(2,1)} %param.7) | copy-start | bytes 786436
  6.5 56.1 %all-gather.3.cloned.1.call-start = ((), (), s32[]{:S(2)}) async-start(), calls=%async_computation.1 | async-start | bytes 2359296 | tf_op jit(solution)/shard_map/all_gather | solution.py:35
  7.3 226.1 %all-gather.5.cloned.1.call-start = ((), (), s32[]{:S(2)}) async-start(), calls=%async_computation.2 | async-start | bytes 9437184 | tf_op jit(solution)/shard_map/all_gather | solution.py:36
  7.3 13.3 %collective-permute-start = (bf16[4,256,256]{2,1,0:T(8,128)(2,1)}, bf16[4,256,256]{2,1,0:T(8,128)(2,1)S(1)}, u32[]{:S(2)}, u32[]{:S(2)}) collective-permute-start(bf16[4,256,256]{2,1,0:T(8,128)(2,1)} %param.8), channel_id=1, source_target_pairs={{120,0},{0,8},{8,16},{16,24},{24,32},{32,40},{40,48},{48,56},{56,6... | collective-permute-start | bytes 1572872 | tf_op jit(solution)/shard_map/ppermute | solution.py:12
  21.8 1.0 copy-start
  22.8 643.3 %reduce-scatter.2.cloned.1.call-start = ((), (), s32[]{:S(2)}) async-start(), calls=%async_computation.3 | async-start | bytes 26738688 | tf_op jit(solution)/shard_map/reduce_scatter | solution.py:52
  22.8 6.9 %collective-permute-start.1 = (bf16[4,256]{1,0:T(4,128)(2,1)}, bf16[4,256]{1,0:T(4,128)(2,1)S(1)}, u32[]{:S(2)}, u32[]{:S(2)}) collective-permute-start(bf16[4,256]{1,0:T(4,128)(2,1)} %param.10), channel_id=1, source_target_pairs={{120,0},{0,8},{8,16},{16,24},{24,32},{32,40},{40,48},{48,56},{56,6... | collective-permute-start | bytes 6152 | tf_op jit(solution)/shard_map/ppermute | solution.py:12
  62.6 6.3 copy-start.2
  73.4 160.0 %copy-start.1 = (bf16[8,256,256]{2,1,0:T(8,128)(2,1)S(1)}, bf16[8,256,256]{2,1,0:T(8,128)(2,1)}, u32[]{:S(2)}) copy-start(bf16[8,256,256]{2,1,0:T(8,128)(2,1)} %copy-done) | copy-start | bytes 3145732
  451.8 3.5 copy-start.7
  451.8 4.1 copy-start.8
  451.8 4.7 copy-start.9
  455.3 2.1 copy-start.4
  455.3 2.7 copy-start.5
  455.3 3.3 copy-start.6
  457.3 2.0 copy-start.3
Sparse Core Ops, SparseCore 0:
  9.0 53.5 all-gather.2
  64.3 169.0 all-gather.4
  470.2 195.8 reduce-scatter.1
where the time goes:
time: 674 us; the launch traced here: 673 us
  waiting for transfers between devices  393 us (58%)
  local copies, waits for them, and re-layouts  126 us (19%)
  other arithmetic  74 us (11%)
  matrix products  65.6 us (10%)
  between operations  13.3 us (2%)
    reduce_scatter x1, waiting for transfers between devices, on_device(): return lax.psum_scatter(partial_chi, 'kpt', scatter_dimension=3, tiled=True)  196 us
    all_gather x1, waiting for transfers between devices, on_device(): lax.all_gather(window, 'row', axis=1, tiled=True)  151 us
    gather x12, local copies, waits for them, and re-layouts, on_device(): virt_green = jnp.take(window_green, window_slots[transfer], axis=0)  121 us
    dot_general x8, matrix products, greens(): jnp.einsum('kri,kci->krc', row_panel, column_panel, preferred_element_typ...  65.6 us
    reduce_sum x1, other arithmetic, on_device(): sums_here.append(jnp.sum(occ_green * virt_green, axis=0))  51.4 us
    all_gather x1, waiting for transfers between devices, on_device(): lax.all_gather(occ_orbitals, 'row', axis=1, tiled=True)  29.8 us
    another operation x5, other arithmetic, on_device(): partial_chi = jnp.stack(blocks, axis=1)  15.6 us
    ppermute x2, waiting for transfers between devices, shifted(): return lax.ppermute(block, axis, route)  15.6 us
  transfers between devices with their start and end apart: 5, of which 5 were waited for; matrix products, arithmetic and copies ran while one was open for 4% of the time, Pallas kernels for 0%

commit v1 on v0

--- a/solution.py
+++ b/solution.py
@@ -4,6 +4,13 @@
 from jax.sharding import PartitionSpec as P
 
 NTAU = 4
+
+
+def all_by_exchange(x, mesh_axis, dim):
+    size = lax.axis_size(mesh_axis)
+    blocks = jnp.stack([x for _ in range(size)])
+    blocks = lax.all_to_all(blocks, mesh_axis, split_axis=0, concat_axis=0)
+    return jnp.concatenate(blocks, axis=dim)
 
 
 def shifted(block, axis, distance):
@@ -33,7 +40,7 @@
     window_gap = jnp.concatenate([earlier_gap, virt_gap], axis=0)
     occ_points, window_points = (
         lax.all_gather(occ_orbitals, "row", axis=1, tiled=True),
-        lax.all_gather(window, "row", axis=1, tiled=True),
+        all_by_exchange(window, "row", 1),
     )
     window_start = (device_k - 1) % kpt_count * local_count
     own_partners = lax.dynamic_slice_in_dim(partner, device_k * local_count, local_count, 1)

time: 674 us -> 626 us (0.929)
  waiting for transfers between devices: 393 us -> 332 us
  local copies, waits for them, and re-layouts: 126 us -> 137 us
    all_gather x1 -> x0, waiting for transfers between devices: 151 us -> none  [on_device(): lax.all_gather(window, 'row', axis=1, tiled=True)]
    ppermute x2, waiting for transfers between devices: 15.6 us -> 114 us  [shifted(): return lax.ppermute(block, axis, route)]
    reshape x0 -> x1, local copies, waits for them, and re-layouts: none -> 7.57 us  [all_by_exchange(): return jnp.concatenate(blocks, axis=dim)]
  transfers between devices with their start and end apart: 5 -> 5, of which waited for: 5 -> 4; matrix products, arithmetic and copies ran while one was open for 4% -> 4% of each run, Pallas kernels for 0% -> 0%
where the time goes in v1:
time: 626 us; the launch traced here: 625 us
  waiting for transfers between devices  332 us (53%)
  local copies, waits for them, and re-layouts  137 us (22%)
  other arithmetic  72 us (12%)
  matrix products  65.5 us (10%)
  between operations  13.6 us (2%)
    reduce_scatter x1, waiting for transfers between devices, on_device(): return lax.psum_scatter(partial_chi, 'kpt', scatter_dimension=3, tiled=True)  192 us
    gather x12, local copies, waits for them, and re-layouts, on_device(): virt_green = jnp.take(window_green, window_slots[transfer], axis=0)  121 us
    ppermute x2, waiting for transfers between devices, shifted(): return lax.ppermute(block, axis, route)  114 us
    dot_general x8, matrix products, greens(): jnp.einsum('kri,kci->krc', row_panel, column_panel, preferred_element_typ...  65.5 us
    reduce_sum x1, other arithmetic, on_device(): sums_here.append(jnp.sum(occ_green * virt_green, axis=0))  51.4 us
    all_gather x1, waiting for transfers between devices, on_device(): lax.all_gather(occ_orbitals, 'row', axis=1, tiled=True)  25 us
    another operation x5, other arithmetic, on_device(): partial_chi = jnp.stack(blocks, axis=1)  15.6 us
  transfers between devices with their start and end apart: 5, of which 4 were waited for; matrix products, arithmetic and copies ran while one was open for 4% of the time, Pallas kernels for 0%

profile of v1, /device:TPU:0, one launch (start us, length us, event | category | flops | bytes accessed | tf_op | source)
XLA Modules:
  0.0 625.1 jit_solution(5882490920319735921)
XLA Ops:
  6.5 13.3 %collective-permute-done = bf16[4,256,256]{2,1,0:T(8,128)(2,1)S(1)} collective-permute-done((bf16[4,256,256]{2,1,0:T(8,128)(2,1)}, bf16[4,256,256]{2,1,0:T(8,128)(2,1)S(1)}, u32[]{:S(2)}, u32[]{:S(2)}) %collective-permute-start) | collective-permute-done | bytes 524320 | tf_op jit(solution)/shard_map/ppermute | solution.py:19
  20.9 4.2 stack.74
  25.2 5.1 all-to-all-start
  31.9 2.4 multiply_exponential_fusion.5
  34.4 100.2 %collective-permute-done.1 = bf16[4,256]{1,0:T(4,128)(2,1)S(1)} collective-permute-done((bf16[4,256]{1,0:T(4,128)(2,1)S(1)}, bf16[4,256]{1,0:T(4,128)(2,1)S(1)}, u32[]{:S(2)}, u32[]{:S(2)}) %collective-permute-start.1) | collective-permute-done | bytes 2080 | tf_op jit(solution)/shard_map/ppermute | solution.py:19
  134.6 2.4 multiply_exponential_fusion.1
  137.1 25.0 %all-gather.2.cloned.1.call-done = bf16[4,2048,128]{2,1,0:T(8,128)(2,1)} async-done(((bf16[4,256,128]{2,1,0:T(8,128)(2,1)}), bf16[4,2048,128]{2,1,0:T(8,128)(2,1)}) %all-gather.2.cloned.1.call-update) | async-done | bytes 2097168 | tf_op jit(solution)/shard_map/all_gather | solution.py:42
  162.0 6.2 fusion.34
  168.2 4.5 fusion.36
  172.7 4.5 fusion.32
  177.1 4.5 fusion.38
  181.6 7.6 %copy.6 = bf16[8,8,256,256]{3,2,1,0:T(8,128)(2,1)} copy(bf16[8,8,256,256]{3,2,0,1:T(8,128)(2,1)} %bitcast.2) | data formatting | bytes 16777216 | tf_op jit(solution)/shard_map/reshape | solution.py:13
  189.2 11.5 %fusion.16 = f32[8,256,2048]{2,1,0:T(8,128)} fusion(bf16[8,2048,256]{2,1,0:T(8,128)(2,1)} %bitcast.43, bf16[8,256,256]{2,1,0:T(8,128)(2,1)S(1)} %constant_dynamic-update-slice_fusion, f32[8,256]{1,0:T(8,128)S(1)} %get-tuple-element.34), kind=kOutput, calls=%fused_computation.49 | convolution fusion | flops 2149056512 | bytes 26222592 | tf_op jit(solution)/shard_map/kri,kci->krc/dot_general | solution.py:28
  200.7 10.0 %gather_fusion.11 = f32[4,256,2048]{2,1,0:T(8,128)} fusion(f32[8,256,2048]{2,1,0:T(8,128)} %fusion.16, s32[1024]{0:T(1024)S(1)} %get-tuple-element.49), kind=kCustom, calls=%fused_computation.11.clone | custom fusion | bytes 16777232 | tf_op jit(solution)/shard_map/jit(_take)/gather | solution.py:55
  210.7 10.1 %gather_fusion.10 = f32[4,256,2048]{2,1,0:T(8,128)} fusion(f32[8,256,2048]{2,1,0:T(8,128)} %fusion.16, s32[1024]{0:T(1024)S(1)} %get-tuple-element.50), kind=kCustom, calls=%fused_computation.10.clone | custom fusion | bytes 16777232 | tf_op jit(solution)/shard_map/jit(_take)/gather | solution.py:55
  220.8 11.5 %fusion.18 = f32[8,256,2048]{2,1,0:T(8,128)} fusion(bf16[8,2048,256]{2,1,0:T(8,128)(2,1)} %bitcast.44, bf16[8,256,256]{2,1,0:T(8,128)(2,1)S(1)} %constant_dynamic-update-slice_fusion, f32[8,256]{1,0:T(8,128)S(1)} %get-tuple-element.33), kind=kOutput, calls=%fused_computation.50 | convolution fusion | flops 2149056512 | bytes 26222592 | tf_op jit(solution)/shard_map/kri,kci->krc/dot_general | solution.py:28
  232.3 10.3 %gather_fusion.8 = f32[4,256,2048]{2,1,0:T(8,128)} fusion(f32[8,256,2048]{2,1,0:T(8,128)} %fusion.18, s32[1024]{0:T(1024)S(1)} %get-tuple-element.49), kind=kCustom, calls=%fused_computation.8.clone | custom fusion | bytes 16777232 | tf_op jit(solution)/shard_map/jit(_take)/gather | solution.py:55
  242.6 10.1 %gather_fusion.7 = f32[4,256,2048]{2,1,0:T(8,128)} fusion(f32[8,256,2048]{2,1,0:T(8,128)} %fusion.18, s32[1024]{0:T(1024)S(1)} %get-tuple-element.50), kind=kCustom, calls=%fused_computation.7.clone | custom fusion | bytes 16777232 | tf_op jit(solution)/shard_map/jit(_take)/gather | solution.py:55
  252.8 10.0 %gather_fusion.9 = f32[4,256,2048]{2,1,0:T(8,128)} fusion(f32[8,256,2048]{2,1,0:T(8,128)} %fusion.16, s32[1024]{0:T(1024)S(1)} %pad_clamp_fusion.2), kind=kCustom, calls=%fused_computation.9.clone | custom fusion | bytes 16777232 | tf_op jit(solution)/shard_map/jit(_take)/gather | solution.py:55
  262.8 10.0 %gather_fusion.6 = f32[4,256,2048]{2,1,0:T(8,128)} fusion(f32[8,256,2048]{2,1,0:T(8,128)} %fusion.18, s32[1024]{0:T(1024)S(1)} %pad_clamp_fusion.2), kind=kCustom, calls=%fused_computation.6.clone | custom fusion | bytes 16777232 | tf_op jit(solution)/shard_map/jit(_take)/gather | solution.py:55
  272.9 11.5 %fusion.22 = f32[8,256,2048]{2,1,0:T(8,128)} fusion(bf16[8,2048,256]{2,1,0:T(8,128)(2,1)} %bitcast.45, bf16[8,256,256]{2,1,0:T(8,128)(2,1)S(1)} %constant_dynamic-update-slice_fusion, f32[8,256]{1,0:T(8,128)S(1)} %get-tuple-element.36), kind=kOutput, calls=%fused_computation.52 | convolution fusion | flops 2149056512 | bytes 26222592 | tf_op jit(solution)/shard_map/kri,kci->krc/dot_general | solution.py:28
  284.4 10.1 %gather_fusion.2 = f32[4,256,2048]{2,1,0:T(8,128)} fusion(f32[8,256,2048]{2,1,0:T(8,128)} %fusion.22, s32[1024]{0:T(1024)S(1)} %get-tuple-element.49), kind=kCustom, calls=%fused_computation.2.clone | custom fusion | bytes 16777232 | tf_op jit(solution)/shard_map/jit(_take)/gather | solution.py:55
  294.4 10.1 %gather_fusion.1 = f32[4,256,2048]{2,1,0:T(8,128)} fusion(f32[8,256,2048]{2,1,0:T(8,128)} %fusion.22, s32[1024]{0:T(1024)S(1)} %get-tuple-element.50), kind=kCustom, calls=%fused_computation.1.clone | custom fusion | bytes 16777232 | tf_op jit(solution)/shard_map/jit(_take)/gather | solution.py:55
  304.5 10.1 %gather_fusion = f32[4,256,2048]{2,1,0:T(8,128)} fusion(f32[8,256,2048]{2,1,0:T(8,128)} %fusion.22, s32[1024]{0:T(1024)S(1)} %pad_clamp_fusion.2), kind=kCustom, calls=%fused_computation.clone | custom fusion | bytes 16777232 | tf_op jit(solution)/shard_map/jit(_take)/gather | solution.py:55
  314.6 11.5 %fusion.20 = f32[8,256,2048]{2,1,0:T(8,128)} fusion(bf16[8,2048,256]{2,1,0:T(8,128)(2,1)} %bitcast.46, bf16[8,256,256]{2,1,0:T(8,128)(2,1)S(1)} %constant_dynamic-update-slice_fusion, f32[8,256]{1,0:T(8,128)S(1)} %get-tuple-element.35), kind=kOutput, calls=%fused_computation.51 | convolution fusion | flops 2149056512 | bytes 26222592 | tf_op jit(solution)/shard_map/kri,kci->krc/dot_general | solution.py:28
  326.1 10.1 %gather_fusion.5 = f32[4,256,2048]{2,1,0:T(8,128)} fusion(f32[8,256,2048]{2,1,0:T(8,128)} %fusion.20, s32[1024]{0:T(1024)S(1)} %get-tuple-element.49), kind=kCustom, calls=%fused_computation.5.clone | custom fusion | bytes 16777232 | tf_op jit(solution)/shard_map/jit(_take)/gather | solution.py:55
  336.2 10.1 %gather_fusion.3 = f32[4,256,2048]{2,1,0:T(8,128)} fusion(f32[8,256,2048]{2,1,0:T(8,128)} %fusion.20, s32[1024]{0:T(1024)S(1)} %pad_clamp_fusion.2), kind=kCustom, calls=%fused_computation.3.clone | custom fusion | bytes 16777232 | tf_op jit(solution)/shard_map/jit(_take)/gather | solution.py:55
  346.2 10.0 %gather_fusion.4 = f32[4,256,2048]{2,1,0:T(8,128)} fusion(f32[8,256,2048]{2,1,0:T(8,128)} %fusion.20, s32[1024]{0:T(1024)S(1)} %get-tuple-element.50), kind=kCustom, calls=%fused_computation.4.clone | custom fusion | bytes 16777232 | tf_op jit(solution)/shard_map/jit(_take)/gather | solution.py:55
  356.3 51.4 %fusion.2 = (f32[256,2048]{1,0:T(8,128)}, f32[256,2048]{1,0:T(8,128)}, f32[256,2048]{1,0:T(8,128)}, f32[256,2048]{1,0:T(8,128)}, f32[256,2048]{1,0:T(8,128)}, /*...) fusion(f32[4,256,2048]{2,1,0:T(8,128)} %fusion.32, ...), kind=kLoop, calls=%fused_computation.18 | loop fusion | flops 69206016 | bytes 159383568 | tf_op jit(solution)/shard_map/reduce_sum | solution.py:56
  407.7 3.4 maximum_bitcast_fusion.3
  417.4 8.5 %pad_maximum_fusion = f32[3,4,256,2048]{3,2,1,0:T(8,128)} fusion(f32[3,1,256,2048]{3,2,1,0:T(8,128)S(1)} %maximum_bitcast_fusion.3, f32[3,1,256,2048]{3,2,1,0:T(8,128)S(1)} %maximum_bitcast_fusion.2, f32[3,1,256,2048]{3,2,1,0:T(8,128)S(1)} %maximum_bitcast_fusion.1, f32[3,1,256,2048]{3,2,1,0:T(8,128)S(1)} %maximum_bitcast_fusion), kind=kLoop, calls=%fused_computation.12 | loop fusion | flops 18874368 | bytes 50331648 | tf_op jit(solution)/shard_map/stack | solution.py:58
  425.9 192.4 %reduce-scatter.2.cloned.1.call-done = f32[3,4,256,128]{3,2,1,0:T(8,128)} async-done(((f32[3,4,256,2048]{3,2,1,0:T(8,128)}), f32[3,4,256,128]{3,2,1,0:T(8,128)}) %reduce-scatter.2.cloned.1.call-update) | async-done | bytes 1572880 | tf_op jit(solution)/shard_map/reduce_scatter | solution.py:59
  (42 shorter events, 8.9 us)
Async XLA Ops:
  6.5 13.3 %collective-permute-start = (bf16[4,256,256]{2,1,0:T(8,128)(2,1)}, bf16[4,256,256]{2,1,0:T(8,128)(2,1)S(1)}, u32[]{:S(2)}, u32[]{:S(2)}) collective-permute-start(bf16[4,256,256]{2,1,0:T(8,128)(2,1)} %param.8), channel_id=1, source_target_pairs={{120,0},{0,8},{8,16},{16,24},{24,32},{32,40},{40,48},{48,56},{56,6... | collective-permute-start | bytes 1572872 | tf_op jit(solution)/shard_map/ppermute | solution.py:19
  25.1 5.9 copy-start.9
  25.2 6.0 copy-start.10
  25.2 6.8 %copy-start.11 = (bf16[4,128]{1,0:T(4,128)(2,1)S(1)}, bf16[4,128]{1,0:T(4,128)(2,1)}, u32[]{:S(2)}) copy-start(bf16[4,128]{1,0:T(4,128)(2,1)} %param.9) | copy-start | bytes 3076
  25.2 136.9 %copy-start.8 = (bf16[4,256,128]{2,1,0:T(8,128)(2,1)S(1)}, bf16[4,256,128]{2,1,0:T(8,128)(2,1)}, u32[]{:S(2)}) copy-start(bf16[4,256,128]{2,1,0:T(8,128)(2,1)} %param.7) | copy-start | bytes 786436
  25.2 156.5 %all-to-all-start = ((bf16[8,8,256,256]{3,2,1,0:T(8,128)(2,1)}), bf16[8,8,256,256]{3,2,1,0:T(8,128)(2,1)}, u32[]{:S(2)}, u32[]{:S(2)}) async-start(bf16[8,8,256,256]{3,2,1,0:T(8,128)(2,1)} %stack.74), calls=%async_computation | async-start | bytes 16777216 | tf_op jit(solution)/shard_map/all_to_all | solution.py:12
  30.3 131.8 %all-gather.2.cloned.1.call-start = ((), (), s32[]{:S(2)}) async-start(), calls=%async_computation.2 | async-start | bytes 2359296 | tf_op jit(solution)/shard_map/all_gather | solution.py:42
  31.0 587.2 %reduce-scatter.2.cloned.1.call-start = ((), (), s32[]{:S(2)}) async-start(), calls=%async_computation.3 | async-start | bytes 26738688 | tf_op jit(solution)/shard_map/reduce_scatter | solution.py:59
  31.1 103.5 %collective-permute-start.1 = (bf16[4,256]{1,0:T(4,128)(2,1)S(1)}, bf16[4,256]{1,0:T(4,128)(2,1)S(1)}, u32[]{:S(2)}, u32[]{:S(2)}) collective-permute-start(bf16[4,256]{1,0:T(4,128)(2,1)S(1)} %copy-done.9), channel_id=1, source_target_pairs={{120,0},{0,8},{8,16},{16,24},{24,32},{32,40},{40,48},{48,56},{56,6... | collective-permute-start | bytes 6152 | tf_op jit(solution)/shard_map/ppermute | solution.py:19
  162.0 6.2 copy-start
  407.7 3.5 copy-start.5
  407.7 4.1 copy-start.6
  407.7 4.7 copy-start.7
  411.1 2.1 copy-start.2
  411.1 2.7 copy-start.3
  411.1 3.3 copy-start.4
  413.2 2.0 copy-start.1
Sparse Core Ops, SparseCore 0:
  32.8 129.2 all-gather.1
  426.0 192.1 reduce-scatter.1
